TPU v7x, 768 devices: a whole 4x8x12 slice. The times are simulated.
768 devices in a mesh: dp: 48 (over z, y_hi, core), fsdp: 16 (over x, y_lo).
Axes of the slice: x: 4, y: 8 (y_hi: 2, y_lo: 4; y = y_hi * 4 + y_lo), z: 12, core: 2. Of those that a mesh axis runs over, the one named last changes fastest.
Arguments:
- acts: bfloat16 [196608, 4096], P(('dp', 'fsdp')), may hold values from -6 to 6
- cotangent: bfloat16 [196608, 4096], P(('dp', 'fsdp')), may hold values from -0.03125 to 0.03125
- projector: bfloat16 [4096, 512], P('fsdp'), may hold values from -0.09375 to 0.09375
- first_moment: float32 [4096, 512], P('fsdp'), may hold values from -4 to 4
- second_moment: float32 [4096, 512], P('fsdp'), may hold values from 0.0005 to 0.005
Outputs:
- first_new: float32 [4096, 512], P('fsdp')
- second_new: float32 [4096, 512], P('fsdp')
- update: float32 [4096, 4096], P(None, 'fsdp')
All inputs are finite; a program needn't handle non-finite values.
Results may differ from a plain program's by a relative error of at most 0.017.
Values may be sent and summed in bfloat16 or wider, within the bound.
A program may use at most 64 MiB of HBM per device.

v0:
```python
import jax
import jax.numpy as jnp
from jax import lax
from jax.sharding import PartitionSpec as P

STEP = 2


def on_device(acts, cotangent, projector, first_moment, second_moment):
    full_proj = lax.all_gather(projector, "fsdp", axis=0, tiled=True)
    coords = jnp.dot(acts, full_proj, preferred_element_type=jnp.float32).astype(jnp.bfloat16)
    grad_part = lax.psum_scatter(
        lax.dot_general(
            cotangent, coords, (((0,), (0,)), ((), ())), preferred_element_type=jnp.float32
        ).astype(jnp.bfloat16),
        "fsdp",
        scatter_dimension=0,
        tiled=True,
    ).astype(jnp.float32)
    grad_low = lax.psum(grad_part, "dp")
    first_new = 0.9 * first_moment + 0.1 * grad_low
    second_new = 0.999 * second_moment + 0.001 * grad_low * grad_low
    first_fix = 1.0 - 0.9**STEP
    second_fix = 1.0 - 0.999**STEP
    direction = (first_new / first_fix / (jnp.sqrt(second_new / second_fix) + 1e-08)).astype(
        jnp.bfloat16
    )
    update = lax.dot_general(
        full_proj, direction, (((1,), (1,)), ((), ())), preferred_element_type=jnp.float32
    )
    return (first_new, second_new, update)


def solution(mesh):
    in_specs = (
        P(("dp", "fsdp"), None),
        P(("dp", "fsdp"), None),
        P("fsdp", None),
        P("fsdp", None),
        P("fsdp", None),
    )
    out_specs = (P("fsdp", None), P("fsdp", None), P(None, "fsdp"))
    return jax.shard_map(
        on_device, mesh=mesh, in_specs=in_specs, out_specs=out_specs, check_vma=False
    )
```

profile of v0, /device:TPU:1, one launch (start us, length us, event | category | flops | bytes accessed | tf_op | source)
XLA Modules:
  0.0 511.1 jit_solution(17060308429942686296)
XLA Ops:
  7.2 0.0 copy-start
  7.2 0.0 all-gather.2.cloned.1.call-start
  7.2 0.7 all-gather.2.cloned.1.call-update
  7.9 0.0 reduce-scatter.2.cloned.1.call-start
  8.0 117.1 %all-gather.2.cloned.1.call-done = bf16[4096,512]{1,0:T(8,128)(2,1)} async-done(((bf16[256,512]{1,0:T(8,128)(2,1)}), bf16[4096,512]{1,0:T(8,128)(2,1)}) %all-gather.2.cloned.1.call-update) | async-done | bytes 4194320 | tf_op jit(solution)/shard_map/all_gather | solution.py:10
  125.0 0.0 copy-done
  125.0 7.3 %fusion = bf16[4096,512]{0,1:T(8,128)(2,1)} fusion(bf16[256,4096]{1,0:T(8,128)(2,1)S(1)} %copy-done, bf16[256,4096]{1,0:T(8,128)(2,1)} %param.5, bf16[4096,512]{1,0:T(8,128)(2,1)} %all-gather.2.cloned.1.call-done), kind=kOutput, calls=%fused_computation.1 | convolution fusion | flops 2149711872 | bytes 12582912 | tf_op jit(solution)/shard_map/dot_general | solution.py:13
  132.4 0.0 copy-start.1
  132.4 0.0 copy-start.2
  132.4 0.0 reduce-scatter.2.cloned.1.call-update
  132.4 1.0 copy-done.1
  133.4 1.0 copy.8
  134.4 0.0 copy-done.2
  134.5 1.0 copy.9
  135.4 100.0 %reduce-scatter.2.cloned.1.call-done = bf16[256,512]{0,1:T(8,128)(2,1)} async-done(((bf16[4096,512]{0,1:T(8,128)(2,1)}), bf16[256,512]{0,1:T(8,128)(2,1)}) %reduce-scatter.2.cloned.1.call-update) | async-done | bytes 262160 | tf_op jit(solution)/shard_map/reduce_scatter | solution.py:12
  235.4 254.1 %all-reduce.1 = f32[256,512]{0,1:T(8,128)} all-reduce(bf16[256,512]{0,1:T(8,128)(2,1)} %reduce-scatter.2.cloned.1.call-done), channel_id=1, replica_groups=mesh['dp'=48,'fsdp'=16] {'dp'}, use_global_device_ids=true, to_apply=%region_1.0 | all-reduce | flops 131072 | bytes 786432 | tf_op jit(solution)/shard_map/psum | solution.py:20
  489.5 1.5 fusion.1
  491.0 1.0 copy.10
  492.0 1.0 copy.11
  493.0 5.6 %convolution_bitcast_fusion = f32[4096,256]{0,1:T(8,128)} fusion(bf16[4096,512]{1,0:T(8,128)(2,1)} %all-gather.2.cloned.1.call-done, f32[256,512]{0,1:T(8,128)S(1)} %get-tuple-element.6, f32[256,512]{0,1:T(8,128)S(1)} %get-tuple-element.7), kind=kOutput, calls=%fused_computation.2 | convolution fusion | flops 1074397184 | bytes 9437184 | tf_op jit(solution)/shard_map/dot_general | solution.py:28
  498.7 5.6 %copy.12 = f32[4096,256]{1,0:T(8,128)} copy(f32[4096,256]{0,1:T(8,128)} %convolution_bitcast_fusion) | data formatting | bytes 8388608
Async XLA Ops:
  7.2 117.9 %copy-start = (bf16[256,4096]{1,0:T(8,128)(2,1)S(1)}, bf16[256,4096]{1,0:T(8,128)(2,1)}, u32[]{:S(2)}) copy-start(bf16[256,4096]{1,0:T(8,128)(2,1)} %param.6) | copy-start | bytes 6291460
  7.2 117.9 %all-gather.2.cloned.1.call-start = ((), (), s32[]{:S(2)}) async-start(), calls=%async_computation.1 | async-start | bytes 4456448 | tf_op jit(solution)/shard_map/all_gather | solution.py:10
  7.9 227.5 %reduce-scatter.2.cloned.1.call-start = ((), (), s32[]{:S(2)}) async-start(), calls=%async_computation.2 | async-start | bytes 4456448 | tf_op jit(solution)/shard_map/reduce_scatter | solution.py:12
  132.4 1.0 copy-start.1
  132.4 2.1 copy-start.2
Sparse Core Ops, SparseCore 0:
  10.4 114.6 all-gather.1
  132.5 102.8 reduce-scatter.1
where the time goes:
time: 521 us; the launch traced here: 511 us
  blocking collectives  254 us (49%)
  waiting for transfers between devices  218 us (42%)
  between operations  14.1 us (3%)
  matrix products  13 us (2%)
  local copies, waits for them, and re-layouts  10.6 us (2%)
    psum x1, blocking collectives, on_device(): grad_low = lax.psum(grad_part, 'dp')  254 us
    all_gather x1, waiting for transfers between devices, on_device(): full_proj = lax.all_gather(projector, 'fsdp', axis=0, tiled=True)  117 us
    reduce_scatter x1, waiting for transfers between devices, on_device(): lax.psum_scatter(lax.dot_general(cotangent, coords, (((0,), (0,)), ((), (...  100 us
    unnamed x11, local copies, waits for them, and re-layouts  10.6 us
  transfers between devices with their start and end apart: 2, of which 2 were waited for; matrix products, arithmetic and copies ran while one was open for 0% of the time, Pallas kernels for 0%

commit v1 on v0

v1 whole, which is shorter than its diff:
```python
import jax
import jax.numpy as jnp
from jax import lax
from jax.experimental import pallas as pl
from jax.experimental.pallas import tpu as pltpu
from jax.sharding import PartitionSpec as P

MESH = pl.DeviceIdType.MESH
STEP = 2
NX, NY, NYL, NZ = 4, 8, 4, 12
BLK = 256
HALF, QUART = 128, 64
PIECE = 48
X, Y = 0, 1
BF16, F32 = jnp.bfloat16, jnp.float32


def gather_reduce(
    acts, cot, proj, pfull, gsum,
    acts_v, cot_v, p_v, acc, coords_t, term_v,
    far1, dir1, comb1, csrc1, mid_v, own2, far2, dir2, comb2, csrc2,
    zb, zrecv, ybuf, gb,
    ld_sem, sib_send, sib_recv, ag_send, ag_recv, out_sem, osib_send, osib_recv,
    rs_send, rs1_recv, rs2_recv, z_send, z_recv, y_sem, g_send, g_recv, fin_sem,
):
    dp, fs = lax.axis_index("dp"), lax.axis_index("fsdp")
    core, y_hi, z = dp % 2, (dp // 2) % 2, dp // 4
    x, y_lo = fs // NYL, fs % NYL
    y = y_hi * NYL + y_lo

    def device(dx=0, dy=0, dz=0, other=False):
        yy = (y + dy + NY) % NY
        xx = (x + dx + NX) % NX
        zz = (z + dz) % NZ
        cc = 1 - core if other else core
        return ((zz * 2 + yy // NYL) * 2 + cc, xx * NYL + yy % NYL)

    sibling = device(other=True)
    near = {(X, 1): device(dx=1), (X, -1): device(dx=-1), (Y, 1): device(dy=1), (Y, -1): device(dy=-1)}
    across = device(dy=4)
    column = [device(dz=k) for k in range(NZ)]
    mine = pl.ds(pl.multiple_of(core * BLK, BLK), BLK)

    def block_of(s):
        return ((x + s // 4) % NX) * NYL + (y_lo + s % 4) % NYL

    def columns(s):
        return pl.ds(pl.multiple_of(block_of(s) * BLK, BLK), BLK)

    own_p = pltpu.make_async_copy(proj.at[:, mine], p_v.at[0], ld_sem.at[2, 0])
    own_p.start()

    def load(s, _):
        pltpu.make_async_copy(acts.at[:, columns(s)], acts_v.at[s, pl.ds(0, BLK)], ld_sem.at[0, s]).start()
        pltpu.make_async_copy(cot.at[:, columns(s)], cot_v.at[s, pl.ds(0, BLK)], ld_sem.at[1, s]).start()
        return 0

    barrier = pltpu.get_barrier_semaphore()
    peers = [sibling, across, *near.values(), *column[1:]]
    for peer in peers:
        pl.semaphore_signal(barrier, inc=1, device_id=peer, device_id_type=MESH)
    lax.fori_loop(0, 16, load, 0)
    zb[pl.ds(512, 64), :] = jnp.zeros((64, 128), BF16)
    acc[...] = jnp.zeros_like(acc)
    pl.semaphore_wait(barrier, len(peers))

    def remote(src, dst, send, recv, target):
        copy = pltpu.make_async_remote_copy(
            src_ref=src, dst_ref=dst, send_sem=send, recv_sem=recv, device_id=target, device_id_type=MESH
        )
        copy.start()
        return copy

    def arrived(ref, sem):
        pltpu.make_async_copy(ref, ref, sem).wait()

    ag_sends = []

    def slot(part, u, v):
        return (u % 4) * 4 + v % 4 if part == 0 else (v % 4) * 4 + u % 4

    def rows(part, half):
        if half is None:
            return pl.ds(part * HALF, HALF)
        return pl.ds(part * HALF + half * QUART, QUART)

    def spread(part, u, v, half, stage, way):
        axis = (X, Y)[part] if stage == 1 else (Y, X)[part]
        s = slot(part, u, v)
        d = slot(part, u - way, v) if stage == 1 else slot(part, u, v - way)
        r = rows(part, half)
        src = proj.at[r, mine] if s == 0 else p_v.at[s, r]
        ag_sends.append(
            remote(
                src, p_v.at[d, r], ag_send.at[len(ag_sends)], ag_recv.at[part, d, half or 0], near[axis, way]
            )
        )

    seen = set()

    def got(part, u, v, half=None):
        s = slot(part, u, v)
        if (part, s, half) not in seen:
            seen.add((part, s, half))
            arrived(p_v.at[s, rows(part, half)], ag_recv.at[part, s, half or 0])

    def gotten(part, u, v):
        if v % 4 == 2:
            got(part, u, v, 0)
            got(part, u, v, 1)
        elif v % 4 != 0:
            got(part, u, v)
        elif u % 4 == 2:
            got(part, u, v, 0)
            got(part, u, v, 1)
        elif u % 4 != 0:
            got(part, u, v)

    def multiply(rx, ry):
        s = (rx % 4) * 4 + ry % 4
        gotten(0, rx, ry)
        gotten(1, ry, rx)
        arrived(acts_v.at[s, pl.ds(0, BLK)], ld_sem.at[0, s])
        arrived(acts_v.at[s, pl.ds(BLK, BLK)], sib_recv.at[0, s])
        acc[...] += jnp.dot(acts_v[s], p_v[s], preferred_element_type=F32)

    for part in (0, 1):
        for stage in (1, 2):
            for way in (1, -1):
                spread(part, 0, 0, None, stage, way)

    def lend(s, _):
        remote(acts.at[:, columns(s)], acts_v.at[s, pl.ds(BLK, BLK)], sib_send.at[0, s], sib_recv.at[0, s], sibling)
        return 0

    def lend_cot(s, _):
        remote(cot.at[:, columns(s)], cot_v.at[s, pl.ds(BLK, BLK)], sib_send.at[1, s], sib_recv.at[1, s], sibling)
        return 0

    lax.fori_loop(0, 16, lend, 0)
    lax.fori_loop(0, 16, lend_cot, 0)
    own_p.wait()

    def relay(part, u):
        gotten(part, u, 3)
        spread(part, u, 3, 0, 2, 1)
        gotten(part, u, 1)
        spread(part, u, 1, 1, 2, -1)

    for part in (0, 1):
        gotten(part, 3, 0)
        spread(part, 3, 0, 0, 1, 1)
        gotten(part, 1, 0)
        spread(part, 1, 0, 1, 1, -1)
    for part in (0, 1):
        for u in (3, 1):
            spread(part, u, 0, None, 2, 1)
            spread(part, u, 0, None, 2, -1)
    for part in (0, 1):
        relay(part, 0)
    multiply(0, 0)
    for part in (0, 1):
        gotten(part, 2, 0)
        spread(part, 2, 0, None, 2, 1)
        spread(part, 2, 0, None, 2, -1)
    for rx, ry in ((1, 0), (3, 0), (0, 1), (0, 3)):
        multiply(rx, ry)
    for u in (3, 1):
        for part in (0, 1):
            relay(part, u)
    for rx, ry in ((1, 1), (1, 3), (3, 1), (3, 3)):
        multiply(rx, ry)
    for part in (0, 1):
        relay(part, 2)
    for rx, ry in ((2, 0), (0, 2), (1, 2), (3, 2), (2, 1), (2, 3), (2, 2)):
        multiply(rx, ry)

    def give(s, _):
        place = pl.ds(pl.multiple_of(block_of(s) * BLK, BLK), BLK)
        pltpu.make_async_copy(p_v.at[s], pfull.at[core, place], out_sem.at[s]).start()
        remote(p_v.at[s], pfull.at[core, place], osib_send.at[s], osib_recv.at[s], sibling)
        return 0

    coords_t[...] = acc[...].astype(BF16).T

    rs_sends = []

    def send(src, dst, sem, axis, way):
        rs_sends.append(remote(src, dst, rs_send.at[len(rs_sends)], sem, near[axis, way]))

    def rs_slot(part, u, v):
        return (v % 4) * 4 + u % 4 if part == 0 else (u % 4) * 4 + v % 4

    def term(s):
        arrived(cot_v.at[s, pl.ds(0, BLK)], ld_sem.at[1, s])
        arrived(cot_v.at[s, pl.ds(BLK, BLK)], sib_recv.at[1, s])
        term_v[s] = jnp.dot(coords_t[...], cot_v[s], preferred_element_type=F32).astype(BF16)

    first = ((Y, X), (X, Y))
    WAYS = ((0, 1), (1, -1))
    done = set()

    def need(part, u, v):
        s = rs_slot(part, u, v)
        if s not in done:
            done.add(s)
            term(s)
        return s

    order = (2, 1, 3, 0)
    for v in order:
        for part in (0, 1):
            s = need(part, 2, v)
            for w, way in WAYS:
                send(term_v.at[s, rows(part, w)], far1.at[part, w, v], rs1_recv.at[0, part, w, v], first[part][0], way)
    for v in order:
        for part in (0, 1):
            for w, way in WAYS:
                s = need(part, way, v)
                send(
                    term_v.at[s, rows(part, 1 - w)], dir1.at[part, w, v], rs1_recv.at[1, part, w, v],
                    first[part][0], way,
                )
    need(0, 0, 0)
    for v in order:
        for part in (0, 1):
            for w, way in WAYS:
                s = rs_slot(part, way, v)
                arrived(far1.at[part, w, v], rs1_recv.at[0, part, w, v])
                csrc1[part, w, v] = (
                    term_v[s, rows(part, w), :].astype(F32) + far1[part, w, v].astype(F32)
                ).astype(BF16)
                send(csrc1.at[part, w, v], comb1.at[part, w, v], rs1_recv.at[2, part, w, v], first[part][0], way)
    lax.fori_loop(0, 16, give, 0)

    def total1(part, v, w):
        s = rs_slot(part, 0, v)
        arrived(comb1.at[part, w, v], rs1_recv.at[2, part, w, v])
        arrived(dir1.at[part, 1 - w, v], rs1_recv.at[1, part, 1 - w, v])
        return (
            term_v[s, rows(part, w), :].astype(F32)
            + comb1[part, w, v].astype(F32)
            + dir1[part, 1 - w, v].astype(F32)
        )

    for v in (2, 1, 3):
        for part in (0, 1):
            for w, way in WAYS:
                mid_v[part, v, pl.ds(w * QUART, QUART), :] = total1(part, v, w).astype(BF16)
                if v == 2:
                    send(
                        mid_v.at[part, v, pl.ds(w * QUART, QUART)], far2.at[part, w], rs2_recv.at[0, part, w],
                        first[part][1], way,
                    )
                elif v % 4 == (-way) % 4:
                    send(
                        mid_v.at[part, v, pl.ds(w * QUART, QUART)], dir2.at[part, 1 - w], rs2_recv.at[1, part, 1 - w],
                        first[part][1], -way,
                    )
    for part in (0, 1):
        for w, way in WAYS:
            own2[part, pl.ds(w * QUART, QUART), :] = total1(part, 0, w)
    for part in (0, 1):
        for w, way in WAYS:
            arrived(far2.at[part, w], rs2_recv.at[0, part, w])
            csrc2[part, w] = (
                mid_v[part, way % 4, pl.ds(w * QUART, QUART), :].astype(F32) + far2[part, w].astype(F32)
            ).astype(BF16)
            send(csrc2.at[part, w], comb2.at[part, w], rs2_recv.at[2, part, w], first[part][1], way)
    for part in (0, 1):
        for w, way in WAYS:
            arrived(comb2.at[part, w], rs2_recv.at[2, part, w])
            arrived(dir2.at[part, 1 - w], rs2_recv.at[1, part, 1 - w])
            total = (
                own2[part, pl.ds(w * QUART, QUART), :]
                + comb2[part, w].astype(F32)
                + dir2[part, 1 - w].astype(F32)
            ).astype(BF16)
            at = part * HALF + w * QUART
            zb[pl.ds(at, QUART), :] = total[:, :128]
            zb[pl.ds(256 + at, QUART), :] = total[:, 128:]

    def piece(k):
        return pl.ds(pl.multiple_of(((z + k) % NZ) * PIECE, 16), PIECE)

    far_first = (6, 5, 7, 4, 8, 3, 9, 2, 10, 1, 11)
    out = [
        remote(zb.at[piece(k)], zrecv.at[k], z_send.at[k], z_recv.at[k], column[k]) for k in far_first
    ]
    part_sum = zb[piece(0), :].astype(F32)
    for k in reversed(far_first):
        arrived(zrecv.at[k], z_recv.at[k])
        part_sum += zrecv[k].astype(F32)
    ybuf[0] = part_sum.astype(BF16)
    swap = remote(ybuf.at[0], ybuf.at[1], y_sem.at[0], y_sem.at[1], across)
    swap.wait()
    gb[piece(0), :] = (ybuf[0].astype(F32) + ybuf[1].astype(F32)).astype(BF16)
    back = [
        remote(gb.at[piece(0)], gb.at[piece(0)], g_send.at[k], g_recv.at[k], column[k]) for k in far_first
    ]
    for k in reversed(far_first):
        arrived(gb.at[piece(NZ - k)], g_recv.at[k])
    keep = pltpu.make_async_copy(gb, gsum.at[core], fin_sem.at[0])
    keep.start()
    tell = remote(gb, gsum.at[core], fin_sem.at[1], fin_sem.at[2], sibling)

    def finish(s, _):
        other = 1 - core
        place = pl.ds(pl.multiple_of(block_of(s) * BLK, BLK), BLK)
        arrived(acts_v.at[s, pl.ds(0, BLK)], sib_send.at[0, s])
        arrived(cot_v.at[s, pl.ds(0, BLK)], sib_send.at[1, s])
        arrived(pfull.at[core, place], out_sem.at[s])
        arrived(p_v.at[s], osib_send.at[s])
        arrived(pfull.at[other, place], osib_recv.at[s])
        return 0

    lax.fori_loop(0, 16, finish, 0)
    for copy in ag_sends + rs_sends + out + back:
        copy.wait_send()
    keep.wait()
    tell.wait_send()
    arrived(gsum.at[1 - core], fin_sem.at[2])


def gather_and_sum(acts, cotangent, projector):
    dma = pltpu.SemaphoreType.DMA
    any_space = pl.BlockSpec(memory_space=pl.ANY)
    return pl.pallas_call(
        gather_reduce,
        out_shape=(
            jax.ShapeDtypeStruct((2, 4096, BLK), BF16),
            jax.ShapeDtypeStruct((2, NZ * PIECE, 128), BF16),
        ),
        in_specs=[any_space] * 3,
        out_specs=(any_space, any_space),
        scratch_shapes=[
            pltpu.VMEM((16, 512, BLK), BF16),
            pltpu.VMEM((16, 512, BLK), BF16),
            pltpu.VMEM((16, BLK, BLK), BF16),
            pltpu.VMEM((512, BLK), F32),
            pltpu.VMEM((BLK, 512), BF16),
            pltpu.VMEM((16, BLK, BLK), BF16),
            pltpu.VMEM((2, 2, 4, QUART, BLK), BF16),
            pltpu.VMEM((2, 2, 4, QUART, BLK), BF16),
            pltpu.VMEM((2, 2, 4, QUART, BLK), BF16),
            pltpu.VMEM((2, 2, 4, QUART, BLK), BF16),
            pltpu.VMEM((2, 4, HALF, BLK), BF16),
            pltpu.VMEM((2, HALF, BLK), F32),
            pltpu.VMEM((2, 2, QUART, BLK), BF16),
            pltpu.VMEM((2, 2, QUART, BLK), BF16),
            pltpu.VMEM((2, 2, QUART, BLK), BF16),
            pltpu.VMEM((2, 2, QUART, BLK), BF16),
            pltpu.VMEM((NZ * PIECE, 128), BF16),
            pltpu.VMEM((NZ, PIECE, 128), BF16),
            pltpu.VMEM((2, PIECE, 128), BF16),
            pltpu.VMEM((NZ * PIECE, 128), BF16),
            dma((3, 16)),
            dma((2, 16)),
            dma((2, 16)),
            dma((48,)),
            dma((2, 16, 2)),
            dma((16,)),
            dma((16,)),
            dma((16,)),
            dma((64,)),
            dma((3, 2, 2, 4)),
            dma((3, 2, 2)),
            dma((NZ,)),
            dma((NZ,)),
            dma((2,)),
            dma((NZ,)),
            dma((NZ,)),
            dma((3,)),
        ],
        compiler_params=pltpu.CompilerParams(
            collective_id=1, has_side_effects=True, vmem_limit_bytes=40 << 20
        ),
        name="gather_and_sum",
    )(acts, cotangent, projector)


def update_kernel(p, g, m1, m2, first_new, second_new, update, direction):
    @pl.when(pl.program_id(0) == 0)
    def _():
        first_fix = 1.0 - 0.9**STEP
        second_fix = 1.0 - 0.999**STEP
        for half in range(2):
            low = jnp.concatenate(
                [g[half, pl.ds(0, 256), :], g[half, pl.ds(256, 256), :]], axis=1
            ).astype(F32).T
            cols = pl.ds(half * BLK, BLK)
            first = 0.9 * m1[:, cols] + 0.1 * low
            second = 0.999 * m2[:, cols] + 0.001 * low * low
            first_new[:, cols] = first
            second_new[:, cols] = second
            direction[half] = (
                first / first_fix / (jnp.sqrt(second / second_fix) + 1e-08)
            ).astype(BF16)

    dims = (((1,), (1,)), ((), ()))
    update[...] = lax.dot_general(
        p[0], direction[0], dims, preferred_element_type=F32
    ) + lax.dot_general(p[1], direction[1], dims, preferred_element_type=F32)


def adam_and_update(pfull, gsum, first_moment, second_moment):
    tile = 512
    whole = pl.BlockSpec((BLK, 512), lambda i: (0, 0))
    return pl.pallas_call(
        update_kernel,
        grid=(4096 // tile,),
        out_shape=(
            jax.ShapeDtypeStruct((BLK, 512), F32),
            jax.ShapeDtypeStruct((BLK, 512), F32),
            jax.ShapeDtypeStruct((4096, BLK), F32),
        ),
        in_specs=[
            pl.BlockSpec((2, tile, BLK), lambda i: (0, i, 0)),
            pl.BlockSpec((2, NZ * PIECE, 128), lambda i: (0, 0, 0)),
            whole,
            whole,
        ],
        out_specs=(whole, whole, pl.BlockSpec((tile, BLK), lambda i: (i, 0))),
        scratch_shapes=[pltpu.VMEM((2, BLK, BLK), BF16)],
        compiler_params=pltpu.CompilerParams(vmem_limit_bytes=32 << 20),
        name="adam_and_update",
    )(pfull, gsum, first_moment, second_moment)


def on_device(acts, cotangent, projector, first_moment, second_moment):
    pfull, gsum = gather_and_sum(acts, cotangent, projector)
    return adam_and_update(pfull, gsum, first_moment, second_moment)


def solution(mesh):
    in_specs = (
        P(("dp", "fsdp"), None),
        P(("dp", "fsdp"), None),
        P("fsdp", None),
        P("fsdp", None),
        P("fsdp", None),
    )
    out_specs = (P("fsdp", None), P("fsdp", None), P(None, "fsdp"))
    return jax.shard_map(
        on_device, mesh=mesh, in_specs=in_specs, out_specs=out_specs, check_vma=False
    )
```

time: 521 us -> 85.9 us (0.16); the launches traced: 511 us -> 85.7 us
  blocking collectives: 254 us -> 0 us
  waiting for transfers between devices: 218 us -> 0 us
  Pallas kernels: 0 us -> 80.9 us
  between operations: 14.1 us -> 0.67 us
  matrix products: 13 us -> 0 us
  local copies, waits for them, and re-layouts: 10.6 us -> 4.13 us
    psum x1 -> x0, blocking collectives: 254 us -> none  [on_device(): grad_low = lax.psum(grad_part, 'dp')]
    all_gather x1 -> x0, waiting for transfers between devices: 117 us -> none  [on_device(): full_proj = lax.all_gather(projector, 'fsdp', axis=0, tiled=True)]
    reduce_scatter x1 -> x0, waiting for transfers between devices: 100 us -> none  [on_device(): lax.psum_scatter(lax.dot_general(cotangent, coords, (((0,), (0,)), ((), (...]
    pallas_call x0 -> x2, Pallas kernels: none -> 80.9 us  [the longest x1 75.3 us: gather_and_sum(): pl.pallas_call(gather_reduce, out_shape=(jax.ShapeDtypeStruct((2, 4096, B...]
    dot_general x2 -> x0, matrix products: 13 us -> none  [the longest x1 7.35 us: on_device(): lax.dot_general(cotangent, coords, (((0,), (0,)), ((), ())), preferred_el...]
    unnamed x11 -> x10, local copies, waits for them, and re-layouts: 10.6 us -> 4.13 us
  transfers between devices with their start and end apart: 2 -> 0, of which waited for: 2 -> 0; matrix products, arithmetic and copies ran while one was open for 0% -> 0% of each run, Pallas kernels for 0% -> 0%
where the time goes in v1:
time: 85.9 us; the launch traced here: 85.7 us
  Pallas kernels  80.9 us (94%)
  local copies, waits for them, and re-layouts  4.13 us (5%)
    pallas_call x1, Pallas kernels, gather_and_sum(): pl.pallas_call(gather_reduce, out_shape=(jax.ShapeDtypeStruct((2, 4096, B...  75.3 us
    pallas_call x1, Pallas kernels, adam_and_update(): pl.pallas_call(update_kernel, grid=(4096 // tile,), out_shape=(jax.ShapeD...  5.65 us
    unnamed x10, local copies, waits for them, and re-layouts  4.13 us

profile of v1, /device:TPU:1, one launch (start us, length us, event | category | flops | bytes accessed | tf_op | source)
XLA Modules:
  0.0 85.7 jit_solution(4699467944147336189)
XLA Ops:
  0.6 0.0 copy-start
  0.6 1.6 %copy-done = bf16[256,4096]{1,0:T(8,128)(2,1)S(1)} copy-done((bf16[256,4096]{1,0:T(8,128)(2,1)S(1)}, bf16[256,4096]{1,0:T(8,128)(2,1)}, u32[]{:S(2)}) %copy-start) | copy-done | bytes 2097176
  2.2 0.0 copy-start.1
  2.2 1.6 %copy-done.1 = bf16[256,4096]{1,0:T(8,128)(2,1)S(1)} copy-done((bf16[256,4096]{1,0:T(8,128)(2,1)S(1)}, bf16[256,4096]{1,0:T(8,128)(2,1)}, u32[]{:S(2)}) %copy-start.1) | copy-done | bytes 2097176
  3.8 0.0 copy-start.4
  3.8 0.9 %copy-done.4 = bf16[256,512]{1,0:T(8,128)(2,1)S(1)} copy-done((bf16[256,512]{1,0:T(8,128)(2,1)S(1)}, bf16[256,512]{1,0:T(8,128)(2,1)}, u32[]{:S(2)}) %copy-start.4) | copy-done | bytes 262168
  4.8 0.0 copy-start.2
  4.8 0.0 copy-start.3
  4.8 75.3 %gather_and_sum.1 = (bf16[2,4096,256]{2,1,0:T(8,128)(2,1)S(1)}, bf16[2,576,128]{2,1,0:T(8,128)(2,1)S(1)}) custom-call(bf16[256,4096]{1,0:T(8,128)(2,1)S(1)} %copy-done, bf16[256,4096]{1,0:T(8,128)(2,1)S(1)} %copy-done.1, bf16[256,512]{1,0:T(8,128)(2,1)S(1)} %copy-done.4), custom_call_target="tpu_custom_call" | custom-call | tf_op jit(solution)/shard_map/gather_and_sum/pallas_call | solution.py:328
  80.0 0.0 copy-done.2
  80.1 0.0 copy-done.3
  80.1 5.6 %adam_and_update.1 = (f32[256,512]{1,0:T(8,128)}, f32[256,512]{1,0:T(8,128)}, f32[4096,256]{1,0:T(8,128)}) custom-call(bf16[2,4096,256]{2,1,0:T(8,128)(2,1)S(1)} %get-tuple-element.5.p, bf16[2,576,128]{2,1,0:T(8,128)(2,1)S(1)} %get-tuple-element.6.g, f32[256,512]{1,0:T(8,128)S(1)} %copy-done.2, f32[256,512]{1,0:T(8,128)S(1)} %copy-done.3), custom_call_target="tpu_custom_call" | custom-call | tf_op jit(solution)/shard_map/adam_and_update/pallas_call | solution.py:409
Async XLA Ops:
  0.6 1.6 %copy-start = (bf16[256,4096]{1,0:T(8,128)(2,1)S(1)}, bf16[256,4096]{1,0:T(8,128)(2,1)}, u32[]{:S(2)}) copy-start(bf16[256,4096]{1,0:T(8,128)(2,1)} %acts.1) | copy-start | bytes 6291460
  2.2 1.6 %copy-start.1 = (bf16[256,4096]{1,0:T(8,128)(2,1)S(1)}, bf16[256,4096]{1,0:T(8,128)(2,1)}, u32[]{:S(2)}) copy-start(bf16[256,4096]{1,0:T(8,128)(2,1)} %cot.1) | copy-start | bytes 6291460
  3.8 0.9 %copy-start.4 = (bf16[256,512]{1,0:T(8,128)(2,1)S(1)}, bf16[256,512]{1,0:T(8,128)(2,1)}, u32[]{:S(2)}) copy-start(bf16[256,512]{1,0:T(8,128)(2,1)} %proj.1) | copy-start | bytes 786436
  4.8 75.3 %copy-start.2 = (f32[256,512]{1,0:T(8,128)S(1)}, f32[256,512]{1,0:T(8,128)}, u32[]{:S(2)}) copy-start(f32[256,512]{1,0:T(8,128)} %m1.1) | copy-start | bytes 1572868
  4.8 75.3 %copy-start.3 = (f32[256,512]{1,0:T(8,128)S(1)}, f32[256,512]{1,0:T(8,128)}, u32[]{:S(2)}) copy-start(f32[256,512]{1,0:T(8,128)} %m2.1) | copy-start | bytes 1572868

commit v2 on v0

v2 whole, which is shorter than its diff:
```python
import jax
import jax.numpy as jnp
from jax import lax
from jax.experimental import pallas as pl
from jax.experimental.pallas import tpu as pltpu
from jax.sharding import PartitionSpec as P

MESH = pl.DeviceIdType.MESH
STEP = 2
NX, NY, NYL, NZ = 4, 8, 4, 12
BLK = 256
HALF, QUART = 128, 64
X, Y = 0, 1
BF16, F32 = jnp.bfloat16, jnp.float32


def gather_reduce(
    acts, cot, proj, p_v, g_big, g_small,
    acts_v, cot_v, acc, coords_t, term_v,
    far1a, dir1a, comb1a, csrc1a, mid_a, own2a, far2a, dir2a, comb2a, csrc2a, zb_a, zrecv_a, ybuf_a,
    far1b, dir1b, comb1b, csrc1b, mid_b, own2b, far2b, dir2b, comb2b, csrc2b, zb_b, zrecv_b, ybuf_b,
    hello, ld_sem, sib_send, sib_recv, ag_send, ag_recv, osib_sem,
    rs_send, rs_recv, z_sem, y_sem, g_sem, fin_sem,
):
    dp, fs = lax.axis_index("dp"), lax.axis_index("fsdp")
    core, y_hi, z = dp % 2, (dp // 2) % 2, dp // 4
    x, y_lo = fs // NYL, fs % NYL
    y = y_hi * NYL + y_lo

    def device(dx=0, dy=0, dz=0, other=False):
        yy = (y + dy + NY) % NY
        xx = (x + dx + NX) % NX
        zz = (z + dz) % NZ
        cc = 1 - core if other else core
        return ((zz * 2 + yy // NYL) * 2 + cc, xx * NYL + yy % NYL)

    sibling = device(other=True)
    near = {(X, 1): device(dx=1), (X, -1): device(dx=-1), (Y, 1): device(dy=1), (Y, -1): device(dy=-1)}
    across = device(dy=4)
    column = [device(dz=k) for k in range(NZ)]
    mine = pl.ds(pl.multiple_of(core * BLK, BLK), BLK)

    def columns(s):
        block = ((x + s // 4) % NX) * NYL + (y_lo + s % 4) % NYL
        return pl.ds(pl.multiple_of(block * BLK, BLK), BLK)

    def load(s, _):
        pltpu.make_async_copy(acts.at[:, columns(s)], acts_v.at[s, pl.ds(0, BLK)], ld_sem.at[0]).start()
        pltpu.make_async_copy(cot.at[:, columns(s)], cot_v.at[s, pl.ds(0, BLK)], ld_sem.at[1]).start()
        return 0

    barrier = pltpu.get_barrier_semaphore()
    peers = [*near.values(), column[1], column[NZ - 1], sibling]
    for peer in peers:
        pl.semaphore_signal(barrier, inc=1, device_id=peer, device_id_type=MESH)
    own_p = pltpu.make_async_copy(proj.at[:, mine], p_v.at[0, 0], ld_sem.at[2])
    own_p.start()
    lax.fori_loop(0, 16, load, 0)
    acc[...] = jnp.zeros_like(acc)
    pl.semaphore_wait(barrier, len(peers))

    chain = [near[Y, 1], near[Y, -1], column[1], column[NZ - 1]]

    def greet(r):
        if r > 0:
            pl.semaphore_wait(hello.at[r - 1], len(chain))
        if r < 5:
            for peer in chain:
                pl.semaphore_signal(hello.at[r], inc=1, device_id=peer, device_id_type=MESH)

    def remote(src, dst, send, recv, target):
        copy = pltpu.make_async_remote_copy(
            src_ref=src, dst_ref=dst, send_sem=send, recv_sem=recv, device_id=target, device_id_type=MESH
        )
        copy.start()
        return copy

    def arrived(ref, sem):
        pltpu.make_async_copy(ref, ref, sem).wait()

    both = (3, 0), (1, 0), (2, 0), (0, 3), (0, 1), (3, 3), (3, 1), (1, 3), (1, 1), (2, 3), (2, 1)

    def group(u, v):
        u, v = u % 4, v % 4
        return both.index((u, v)) if (u, v) in both else len(both) + (u == 2)

    def slot(part, u, v):
        return (u % 4) * 4 + v % 4 if part == 0 else (v % 4) * 4 + u % 4

    def rows(part, half):
        if half is None:
            return pl.ds(part * HALF, HALF)
        return pl.ds(part * HALF + half * QUART, QUART)

    def spread(part, u, v, half, stage, way):
        axis = (X, Y)[part] if stage == 1 else (Y, X)[part]
        s = slot(part, u, v)
        d = slot(part, u - way, v) if stage == 1 else slot(part, u, v - way)
        r = rows(part, half)
        src = proj.at[r, mine] if s == 0 else p_v.at[0, s, r]
        at = (u - way, v) if stage == 1 else (u, v - way)
        remote(src, p_v.at[0, d, r], ag_send.at[0], ag_recv.at[group(*at)], near[axis, way])

    seen = set()

    def gotten(u, v):
        if (u % 4, v % 4) == (0, 0):
            return
        g = group(u, v)
        if g not in seen:
            seen.add(g)
            arrived(p_v.at[0, pl.ds(0, 3 if g == len(both) else 1)], ag_recv.at[g])

    def multiply(rx, ry):
        s = (rx % 4) * 4 + ry % 4
        gotten(rx, ry)
        gotten(ry, rx)
        acc[...] += jnp.dot(acts_v[s], p_v[0, s], preferred_element_type=F32)

    for part in (0, 1):
        for way in (1, -1):
            spread(part, 0, 0, None, 1, way)
    for part in (0, 1):
        for way in (1, -1):
            spread(part, 0, 0, None, 2, way)
    greet(0)

    def lend(s, _):
        remote(acts.at[:, columns(s)], acts_v.at[s, pl.ds(BLK, BLK)], sib_send.at[0], sib_recv.at[0], sibling)
        return 0

    def lend_cot(s, _):
        remote(cot.at[:, columns(s)], cot_v.at[s, pl.ds(BLK, BLK)], sib_send.at[1], sib_recv.at[1], sibling)
        return 0

    def give(s, _):
        remote(p_v.at[0, s], p_v.at[1, s], osib_sem.at[0], osib_sem.at[1], sibling)
        return 0

    lax.fori_loop(0, 16, lend, 0)
    own_p.wait()

    def relay(part, u):
        gotten(u, 3)
        spread(part, u, 3, 0, 2, 1)
        gotten(u, 1)
        spread(part, u, 1, 1, 2, -1)

    for part in (0, 1):
        gotten(3, 0)
        spread(part, 3, 0, 0, 1, 1)
        gotten(1, 0)
        spread(part, 1, 0, 1, 1, -1)
    for part in (0, 1):
        for u in (3, 1):
            spread(part, u, 0, None, 2, 1)
            spread(part, u, 0, None, 2, -1)
    lax.fori_loop(0, 16, lend_cot, 0)
    for part in (0, 1):
        relay(part, 0)
    greet(1)
    arrived(acts_v.at[:, pl.ds(0, BLK)], ld_sem.at[0])
    arrived(acts_v.at[:, pl.ds(BLK, BLK)], sib_recv.at[0])
    multiply(0, 0)
    for part in (0, 1):
        gotten(2, 0)
        spread(part, 2, 0, None, 2, 1)
        spread(part, 2, 0, None, 2, -1)
    greet(2)
    for rx, ry in ((1, 0), (3, 0), (0, 1), (0, 3)):
        multiply(rx, ry)
    for u in (3, 1):
        for part in (0, 1):
            relay(part, u)
    greet(3)
    for rx, ry in ((2, 0), (0, 2), (1, 1), (1, 3), (3, 1), (3, 3)):
        multiply(rx, ry)
    for part in (0, 1):
        relay(part, 2)
    greet(4)
    for rx, ry in ((1, 2), (3, 2), (2, 1), (2, 3), (2, 2)):
        multiply(rx, ry)

    coords_t[...] = acc[...].astype(BF16).T
    arrived(cot_v.at[:, pl.ds(0, BLK)], ld_sem.at[1])
    arrived(cot_v.at[:, pl.ds(BLK, BLK)], sib_recv.at[1])

    first = ((Y, X), (X, Y))
    WAYS = ((0, 1), (1, -1))
    order = (2, 1, 3, 0)

    def rs_slot(part, u, v):
        return (v % 4) * 4 + u % 4 if part == 0 else (u % 4) * 4 + v % 4

    done = set()

    def need(part, u, v):
        s = rs_slot(part, u, v)
        if s not in done:
            done.add(s)
            term_v[s] = jnp.dot(coords_t[...], cot_v[s], preferred_element_type=F32).astype(BF16)
        return s

    class Run:
        def __init__(self, index, low, q, buffers):
            self.index, self.low, self.q, self.seen = index, low, q, set()
            (
                self.far1, self.dir1, self.comb1, self.csrc1, self.mid, self.own2,
                self.far2, self.dir2, self.comb2, self.csrc2, self.zb, self.zrecv, self.ybuf,
            ) = buffers

        def send(self, src, dst, kind, v, axis, way):
            recv = rs_recv.at[self.index, kind * 4 + v if kind < 3 else 9 + kind]
            remote(src, dst, rs_send.at[self.index, kind], recv, near[axis, way])

        def came(self, kind, v=None):
            if (kind, v) in self.seen:
                return
            self.seen.add((kind, v))
            buffer = (self.far1, self.dir1, self.comb1, self.far2, self.dir2, self.comb2)[kind]
            if kind < 3:
                arrived(buffer.at[:, :, v], rs_recv.at[self.index, kind * 4 + v])
            else:
                arrived(buffer, rs_recv.at[self.index, 9 + kind])

        def rows(self, part, half):
            return pl.ds(self.low + (2 * part + half) * self.q, self.q)

        def half(self, w):
            return pl.ds(w * self.q, self.q)

        def far(self):
            for v in order:
                for part in (0, 1):
                    s = need(part, 2, v)
                    for w, way in WAYS:
                        self.send(
                            term_v.at[s, self.rows(part, w)], self.far1.at[part, w, v],
                            0, v, first[part][0], way,
                        )

        def direct(self):
            for v in order:
                for part in (0, 1):
                    for w, way in WAYS:
                        s = need(part, way, v)
                        self.send(
                            term_v.at[s, self.rows(part, 1 - w)], self.dir1.at[part, w, v],
                            1, v, first[part][0], way,
                        )

        def combine(self):
            for v in order:
                for part in (0, 1):
                    for w, way in WAYS:
                        s = rs_slot(part, way, v)
                        self.came(0, v)
                        self.csrc1[part, w, v] = (
                            term_v[s, self.rows(part, w), :].astype(F32) + self.far1[part, w, v].astype(F32)
                        ).astype(BF16)
                        self.send(
                            self.csrc1.at[part, w, v], self.comb1.at[part, w, v],
                            2, v, first[part][0], way,
                        )

        def total1(self, part, v, w):
            s = rs_slot(part, 0, v)
            self.came(2, v)
            self.came(1, v)
            return (
                term_v[s, self.rows(part, w), :].astype(F32)
                + self.comb1[part, w, v].astype(F32)
                + self.dir1[part, 1 - w, v].astype(F32)
            )

        def middle(self):
            for v in (2, 1, 3):
                for part in (0, 1):
                    for w, way in WAYS:
                        self.mid[part, v, self.half(w), :] = self.total1(part, v, w).astype(BF16)
                        src = self.mid.at[part, v, self.half(w)]
                        if v == 2:
                            self.send(
                                src, self.far2.at[part, w], 3, 0, first[part][1], way
                            )
                        elif v % 4 == (-way) % 4:
                            self.send(
                                src, self.dir2.at[part, 1 - w], 4, 0, first[part][1], -way
                            )

        def own(self):
            for part in (0, 1):
                for w, _ in WAYS:
                    self.own2[part, self.half(w), :] = self.total1(part, 0, w)

        def combine2(self):
            for part in (0, 1):
                for w, way in WAYS:
                    self.came(3)
                    self.csrc2[part, w] = (
                        self.mid[part, way % 4, self.half(w), :].astype(F32) + self.far2[part, w].astype(F32)
                    ).astype(BF16)
                    self.send(
                        self.csrc2.at[part, w], self.comb2.at[part, w], 5, 0, first[part][1], way
                    )

        def total2(self):
            for part in (0, 1):
                for w, _ in WAYS:
                    self.came(5)
                    self.came(4)
                    total = (
                        self.own2[part, self.half(w), :]
                        + self.comb2[part, w].astype(F32)
                        + self.dir2[part, 1 - w].astype(F32)
                    ).astype(BF16)
                    at = (2 * part + w) * self.q
                    if self.index == 0:
                        self.zb[pl.ds(at, self.q), :] = total
                    else:
                        self.zb[pl.ds(at, self.q), :] = total[:, :128]
                        self.zb[pl.ds(64 + at, self.q), :] = total[:, 128:]

    big = Run(
        0, 0, 48,
        (far1a, dir1a, comb1a, csrc1a, mid_a, own2a, far2a, dir2a, comb2a, csrc2a, zb_a, zrecv_a, ybuf_a),
    )
    small = Run(
        1, 192, 16,
        (far1b, dir1b, comb1b, csrc1b, mid_b, own2b, far2b, dir2b, comb2b, csrc2b, zb_b, zrecv_b, ybuf_b),
    )

    far_first = (6, 5, 7, 4, 8, 3, 9, 2, 10, 1, 11)

    def piece(run, k):
        index = (z + k) % NZ if run.index == 0 else (z + k + 4) % NZ
        return pl.ds(pl.multiple_of(index * 16, 16), 16), index

    def owned(run, k, body):
        if run.index == 0:
            body()
        else:
            pl.when((z + k + 4) % NZ < 8)(body)

    def scatter(run):
        for k in far_first:

            def body(k=k):
                at, _ = piece(run, k)
                remote(run.zb.at[at], run.zrecv.at[k], z_sem.at[run.index, 0], z_sem.at[run.index, 1], column[k])

            owned(run, k, body)

    def swap(run):
        def body():
            at, _ = piece(run, 0)
            part_sum = run.zb[at, :].astype(F32)
            arrived(run.zrecv.at[pl.ds(1, NZ - 1)], z_sem.at[run.index, 1])
            for k in range(1, NZ):
                part_sum += run.zrecv[k].astype(F32)
            run.ybuf[0] = part_sum.astype(BF16)
            remote(run.ybuf.at[0], run.ybuf.at[1], y_sem.at[run.index, 0], y_sem.at[run.index, 1], across)

        owned(run, 0, body)

    def hand_out(run, result):
        def body():
            at, _ = piece(run, 0)
            arrived(run.ybuf.at[1], y_sem.at[run.index, 1])
            result[0, at, :] = (run.ybuf[0].astype(F32) + run.ybuf[1].astype(F32)).astype(BF16)
            for k in far_first:
                remote(result.at[0, at], result.at[0, at], g_sem.at[run.index, 0], g_sem.at[run.index, 1], column[k])

        owned(run, 0, body)

    def others(run, body):
        if run.index == 0:
            body(NZ - 1)
        else:
            pl.when((z + 4) % NZ < 8)(lambda: body(7))
            pl.when((z + 4) % NZ >= 8)(lambda: body(8))

    def collect(run, result):
        others(run, lambda n: arrived(run.zrecv.at[pl.ds(0, n)], g_sem.at[run.index, 1]))
        return remote(
            result.at[0], result.at[1], fin_sem.at[run.index, 0], fin_sem.at[run.index, 1], sibling
        )

    big.far()
    big.direct()
    need(0, 0, 0)
    small.far()
    big.combine()
    small.direct()
    greet(5)
    big.middle()
    small.combine()
    big.own()
    big.combine2()
    lax.fori_loop(0, 16, give, 0)
    small.middle()
    big.total2()
    scatter(big)
    small.own()
    small.combine2()
    small.total2()
    scatter(small)
    swap(big)
    swap(small)
    hand_out(big, g_big)
    hand_out(small, g_small)
    tell = [collect(big, g_big), collect(small, g_small)]

    arrived(acts_v.at[:, pl.ds(0, BLK)], sib_send.at[0])
    arrived(cot_v.at[:, pl.ds(0, BLK)], sib_send.at[1])
    arrived(p_v.at[0], osib_sem.at[0])
    arrived(p_v.at[1], osib_sem.at[1])
    arrived(p_v.at[0, pl.ds(0, 15)], ag_send.at[0])
    for run in (big, small):
        for kind, buffer in enumerate((run.far1, run.dir1, run.comb1, run.far2, run.dir2, run.comb2)):
            arrived(buffer, rs_send.at[run.index, kind])
        others(run, lambda n, run=run: arrived(run.zrecv.at[pl.ds(0, n)], z_sem.at[run.index, 0]))

        def body(run=run):
            arrived(run.ybuf.at[0], y_sem.at[run.index, 0])
            arrived(run.zrecv.at[pl.ds(0, NZ - 1)], g_sem.at[run.index, 0])

        owned(run, 0, body)
    for copy in tell:
        copy.wait()


def gather_and_sum(acts, cotangent, projector):
    dma = pltpu.SemaphoreType.DMA
    hbm = pl.BlockSpec(memory_space=pltpu.HBM)
    vmem = pl.BlockSpec(memory_space=pltpu.VMEM)

    def run_buffers(q, cols, pieces):
        first_stage = [pltpu.VMEM((2, 2, 4, q, BLK), BF16)] * 4
        second_stage = [pltpu.VMEM((2, 2, q, BLK), BF16)] * 4
        return [
            *first_stage,
            pltpu.VMEM((2, 4, 2 * q, BLK), BF16),
            pltpu.VMEM((2, 2 * q, BLK), F32),
            *second_stage,
            pltpu.VMEM((pieces * 16, cols), BF16),
            pltpu.VMEM((NZ, 16, cols), BF16),
            pltpu.VMEM((2, 16, cols), BF16),
        ]

    return pl.pallas_call(
        gather_reduce,
        out_shape=(
            pltpu.VMEM((2, 16, BLK, BLK), BF16),
            pltpu.VMEM((2, 192, BLK), BF16),
            pltpu.VMEM((2, 128, 128), BF16),
        ),
        in_specs=[hbm] * 3,
        out_specs=(vmem, vmem, vmem),
        scratch_shapes=[
            pltpu.VMEM((16, 512, BLK), BF16),
            pltpu.VMEM((16, 512, BLK), BF16),
            pltpu.VMEM((512, BLK), F32),
            pltpu.VMEM((BLK, 512), BF16),
            pltpu.VMEM((16, BLK, BLK), BF16),
            *run_buffers(48, BLK, 12),
            *run_buffers(16, 128, 8),
            pltpu.SemaphoreType.REGULAR((5,)),
            dma((3,)),
            dma((2,)),
            dma((2,)),
            dma((1,)),
            dma((13,)),
            dma((2,)),
            dma((2, 6)),
            dma((2, 15)),
            dma((2, 2)),
            dma((2, 2)),
            dma((2, 2)),
            dma((2, 2)),
        ],
        compiler_params=pltpu.CompilerParams(
            collective_id=1, has_side_effects=True, vmem_limit_bytes=32 << 20
        ),
        name="gather_and_sum",
    )(acts, cotangent, projector)


def update_kernel(p, g_big, g_small, m1, m2, first_new, second_new, update, first_v, second_v, dir_t, update_v, sems):
    core = lax.axis_index("dp") % 2
    fs = lax.axis_index("fsdp")
    x, y_lo = fs // NYL, fs % NYL
    first_fix = 1.0 - 0.9**STEP
    second_fix = 1.0 - 0.999**STEP
    for half in range(2):
        small = g_small[half]
        low = jnp.concatenate(
            [g_big[half], jnp.concatenate([small[:64], small[64:]], axis=1)], axis=0
        ).astype(F32).T
        which = core if half == 0 else 1 - core
        cols = pl.ds(pl.multiple_of(which * BLK, BLK), BLK)
        first = 0.9 * m1[:, cols] + 0.1 * low
        second = 0.999 * m2[:, cols] + 0.001 * low * low
        first_v[:, cols] = first
        second_v[:, cols] = second
        direction = (first / first_fix / (jnp.sqrt(second / second_fix) + 1e-08)).astype(BF16)
        dir_t[half] = direction.T
    moments = [
        pltpu.make_async_copy(first_v, first_new, sems.at[0]),
        pltpu.make_async_copy(second_v, second_new, sems.at[1]),
    ]
    for copy in moments:
        copy.start()
    for s in range(16):
        update_v[s] = jnp.dot(p[0, s], dir_t[0], preferred_element_type=F32) + jnp.dot(
            p[1, s], dir_t[1], preferred_element_type=F32
        )
        block = ((x + s // 4) % NX) * NYL + (y_lo + s % 4) % NYL
        place = pl.ds(pl.multiple_of(block * BLK, BLK), BLK)
        pltpu.make_async_copy(update_v.at[s], update.at[place], sems.at[2]).start()
    for copy in moments:
        copy.wait()
    pltpu.make_async_copy(update_v, update_v, sems.at[2]).wait()


def adam_and_update(p, g_big, g_small, first_moment, second_moment):
    vmem = pl.BlockSpec(memory_space=pltpu.VMEM)
    return pl.pallas_call(
        update_kernel,
        out_shape=(
            jax.ShapeDtypeStruct((BLK, 512), F32),
            jax.ShapeDtypeStruct((BLK, 512), F32),
            jax.ShapeDtypeStruct((4096, BLK), F32),
        ),
        in_specs=[vmem] * 5,
        out_specs=(pl.BlockSpec(memory_space=pl.ANY),) * 3,
        scratch_shapes=[
            pltpu.VMEM((BLK, 512), F32),
            pltpu.VMEM((BLK, 512), F32),
            pltpu.VMEM((2, BLK, BLK), BF16),
            pltpu.VMEM((16, BLK, BLK), F32),
            pltpu.SemaphoreType.DMA((3,)),
        ],
        compiler_params=pltpu.CompilerParams(vmem_limit_bytes=40 << 20),
        name="adam_and_update",
    )(p, g_big, g_small, first_moment, second_moment)


def on_device(acts, cotangent, projector, first_moment, second_moment):
    p, g_big, g_small = gather_and_sum(
        *(pltpu.with_memory_space_constraint(a, pltpu.HBM) for a in (acts, cotangent, projector))
    )
    return adam_and_update(p, g_big, g_small, first_moment, second_moment)


def solution(mesh):
    in_specs = (
        P(("dp", "fsdp"), None),
        P(("dp", "fsdp"), None),
        P("fsdp", None),
        P("fsdp", None),
        P("fsdp", None),
    )
    out_specs = (P("fsdp", None), P("fsdp", None), P(None, "fsdp"))
    return jax.shard_map(
        on_device, mesh=mesh, in_specs=in_specs, out_specs=out_specs, check_vma=False
    )
```

time: 521 us -> 76.4 us (0.15); the launches traced: 511 us -> 76.3 us
  blocking collectives: 254 us -> 0 us
  waiting for transfers between devices: 218 us -> 0 us
  Pallas kernels: 0 us -> 75.6 us
  between operations: 14.1 us -> 0.67 us
  matrix products: 13 us -> 0 us
  local copies, waits for them, and re-layouts: 10.6 us -> 0.01 us
    psum x1 -> x0, blocking collectives: 254 us -> none  [on_device(): grad_low = lax.psum(grad_part, 'dp')]
    all_gather x1 -> x0, waiting for transfers between devices: 117 us -> none  [on_device(): full_proj = lax.all_gather(projector, 'fsdp', axis=0, tiled=True)]
    reduce_scatter x1 -> x0, waiting for transfers between devices: 100 us -> none  [on_device(): lax.psum_scatter(lax.dot_general(cotangent, coords, (((0,), (0,)), ((), (...]
    pallas_call x0 -> x2, Pallas kernels: none -> 75.6 us  [the longest x1 72.7 us: gather_and_sum(): pl.pallas_call(gather_reduce, out_shape=(pltpu.VMEM((2, 16, BLK, BLK), BF...]
    dot_general x2 -> x0, matrix products: 13 us -> none  [the longest x1 7.35 us: on_device(): lax.dot_general(cotangent, coords, (((0,), (0,)), ((), ())), preferred_el...]
    unnamed x11 -> x4, local copies, waits for them, and re-layouts: 10.6 us -> 0.01 us
  transfers between devices with their start and end apart: 2 -> 0, of which waited for: 2 -> 0; matrix products, arithmetic and copies ran while one was open for 0% -> 0% of each run, Pallas kernels for 0% -> 0%
where the time goes in v2:
time: 76.4 us; the launch traced here: 76.3 us
  Pallas kernels  75.6 us (99%)
    pallas_call x1, Pallas kernels, gather_and_sum(): pl.pallas_call(gather_reduce, out_shape=(pltpu.VMEM((2, 16, BLK, BLK), BF...  72.7 us
    pallas_call x1, Pallas kernels, adam_and_update(): pl.pallas_call(update_kernel, out_shape=(jax.ShapeDtypeStruct((BLK, 512),...  2.95 us

profile of v2, /device:TPU:1, one launch (start us, length us, event | category | flops | bytes accessed | tf_op | source)
XLA Modules:
  0.0 76.3 jit_solution(17165288263916472258)
XLA Ops:
  0.6 0.0 copy-start.1
  0.6 0.0 copy-start
  0.7 72.7 %gather_and_sum.1 = (bf16[2,16,256,256]{3,2,1,0:T(8,128)(2,1)S(1)}, bf16[2,192,256]{2,1,0:T(8,128)(2,1)S(1)}, bf16[2,128,128]{2,1,0:T(8,128)(2,1)S(1)}) custom-call(bf16[256,4096]{1,0:T(8,128)(2,1)} %acts.1, bf16[256,4096]{1,0:T(8,128)(2,1)} %cot.1, bf16[256,512]{1,0:T(8,128)(2,1)} %proj.1), custom_call_target="tpu_custom_call" | custom-call | tf_op jit(solution)/shard_map/gather_and_sum/pallas_call | solution.py:451
  73.3 0.0 copy-done.1
  73.4 0.0 copy-done
  73.4 2.9 %adam_and_update.1 = (f32[256,512]{1,0:T(8,128)}, f32[256,512]{1,0:T(8,128)}, f32[4096,256]{1,0:T(8,128)}) custom-call(bf16[2,16,256,256]{3,2,1,0:T(8,128)(2,1)S(1)} %get-tuple-element.6.p, bf16[2,192,256]{2,1,0:T(8,128)(2,1)S(1)} %get-tuple-element.7.g_big, bf16[2,128,128]{2,1,0:T(8,128)(2,1)S(1)} %get-tuple-element.8.g_small, f32[256,512]{1,0:T(8,128)S(1)} %copy-done, ...), custom_call_target="tpu_custom_call" | custom-call | tf_op jit(solution)/shard_map/adam_and_update/pallas_call | solution.py:528
Async XLA Ops:
  0.6 72.7 %copy-start.1 = (f32[256,512]{1,0:T(8,128)S(1)}, f32[256,512]{1,0:T(8,128)}, u32[]{:S(2)}) copy-start(f32[256,512]{1,0:T(8,128)} %m2.1) | copy-start | bytes 1572868
  0.6 72.7 %copy-start = (f32[256,512]{1,0:T(8,128)S(1)}, f32[256,512]{1,0:T(8,128)}, u32[]{:S(2)}) copy-start(f32[256,512]{1,0:T(8,128)} %m1.1) | copy-start | bytes 1572868

commit v3 on v2

--- a/solution.py
+++ b/solution.py
@@ -15,7 +15,7 @@
 
 
 def gather_reduce(
-    acts, cot, proj, p_v, g_big, g_small,
+    acts, cot, proj, p_v, g_v,
     acts_v, cot_v, acc, coords_t, term_v,
     far1a, dir1a, comb1a, csrc1a, mid_a, own2a, far2a, dir2a, comb2a, csrc2a, zb_a, zrecv_a, ybuf_a,
     far1b, dir1b, comb1b, csrc1b, mid_b, own2b, far2b, dir2b, comb2b, csrc2b, zb_b, zrecv_b, ybuf_b,
@@ -39,6 +39,7 @@
     across = device(dy=4)
     column = [device(dz=k) for k in range(NZ)]
     mine = pl.ds(pl.multiple_of(core * BLK, BLK), BLK)
+    ranks = [pl.ds(c * HALF, HALF) for c in (0, 1)]
 
     def columns(s):
         block = ((x + s // 4) % NX) * NYL + (y_lo + s % 4) % NYL
@@ -55,7 +56,6 @@
         pl.semaphore_signal(barrier, inc=1, device_id=peer, device_id_type=MESH)
     own_p = pltpu.make_async_copy(proj.at[:, mine], p_v.at[0, 0], ld_sem.at[2])
     own_p.start()
-    lax.fori_loop(0, 16, load, 0)
     acc[...] = jnp.zeros_like(acc)
     pl.semaphore_wait(barrier, len(peers))
 
@@ -92,38 +92,68 @@
             return pl.ds(part * HALF, HALF)
         return pl.ds(part * HALF + half * QUART, QUART)
 
-    def spread(part, u, v, half, stage, way):
-        axis = (X, Y)[part] if stage == 1 else (Y, X)[part]
-        s = slot(part, u, v)
-        d = slot(part, u - way, v) if stage == 1 else slot(part, u, v - way)
-        r = rows(part, half)
-        src = proj.at[r, mine] if s == 0 else p_v.at[0, s, r]
-        at = (u - way, v) if stage == 1 else (u, v - way)
-        remote(src, p_v.at[0, d, r], ag_send.at[0], ag_recv.at[group(*at)], near[axis, way])
-
-    seen = set()
-
-    def gotten(u, v):
-        if (u % 4, v % 4) == (0, 0):
-            return
-        g = group(u, v)
-        if g not in seen:
-            seen.add(g)
-            arrived(p_v.at[0, pl.ds(0, 3 if g == len(both) else 1)], ag_recv.at[g])
-
-    def multiply(rx, ry):
-        s = (rx % 4) * 4 + ry % 4
-        gotten(rx, ry)
-        gotten(ry, rx)
-        acc[...] += jnp.dot(acts_v[s], p_v[0, s], preferred_element_type=F32)
-
-    for part in (0, 1):
-        for way in (1, -1):
-            spread(part, 0, 0, None, 1, way)
-    for part in (0, 1):
-        for way in (1, -1):
-            spread(part, 0, 0, None, 2, way)
-    greet(0)
+    class Gather:
+        def __init__(self, c):
+            self.c, self.seen = c, set()
+
+        def spread(self, part, u, v, half, stage, way):
+            axis = (X, Y)[part] if stage == 1 else (Y, X)[part]
+            s = slot(part, u, v)
+            at = (u - way, v) if stage == 1 else (u, v - way)
+            r = rows(part, half)
+            if s == 0:
+                src = proj.at[r, pl.ds(pl.multiple_of(core * BLK + self.c * HALF, HALF), HALF)]
+            else:
+                src = p_v.at[0, s, r, ranks[self.c]]
+            dst = p_v.at[0, slot(part, *at), r, ranks[self.c]]
+            remote(src, dst, ag_send.at[self.c], ag_recv.at[self.c, group(*at)], near[axis, way])
+
+        def gotten(self, u, v):
+            if (u % 4, v % 4) == (0, 0):
+                return
+            g = group(u, v)
+            if g not in self.seen:
+                self.seen.add(g)
+                n = 3 if g == len(both) else 1
+                arrived(p_v.at[0, pl.ds(0, n), :, ranks[self.c]], ag_recv.at[self.c, g])
+
+        def own(self):
+            for stage in (1, 2):
+                for part in (0, 1):
+                    for way in (1, -1):
+                        self.spread(part, 0, 0, None, stage, way)
+
+        def beside(self):
+            for u, half, way in ((3, 0, 1), (1, 1, -1)):
+                self.gotten(u, 0)
+                for part in (0, 1):
+                    self.spread(part, u, 0, half, 1, way)
+            for part in (0, 1):
+                for u in (3, 1):
+                    self.spread(part, u, 0, None, 2, 1)
+                    self.spread(part, u, 0, None, 2, -1)
+
+        def relay(self, u):
+            for v, half, way in ((3, 0, 1), (1, 1, -1)):
+                self.gotten(u, v)
+                for part in (0, 1):
+                    self.spread(part, u, v, half, 2, way)
+
+        def opposite(self):
+            self.gotten(2, 0)
+            for part in (0, 1):
+                self.spread(part, 2, 0, None, 2, 1)
+                self.spread(part, 2, 0, None, 2, -1)
+
+        def multiply(self, *places):
+            for rx, ry in places:
+                s = (rx % 4) * 4 + ry % 4
+                self.gotten(rx, ry)
+                self.gotten(ry, rx)
+                acc[self.c] += jnp.dot(acts_v[s], p_v[0, s, :, ranks[self.c]], preferred_element_type=F32)
+
+        def finish(self):
+            coords_t[self.c] = acc[self.c].astype(BF16).T
 
     def lend(s, _):
         remote(acts.at[:, columns(s)], acts_v.at[s, pl.ds(BLK, BLK)], sib_send.at[0], sib_recv.at[0], sibling)
@@ -137,54 +167,6 @@
         remote(p_v.at[0, s], p_v.at[1, s], osib_sem.at[0], osib_sem.at[1], sibling)
         return 0
 
-    lax.fori_loop(0, 16, lend, 0)
-    own_p.wait()
-
-    def relay(part, u):
-        gotten(u, 3)
-        spread(part, u, 3, 0, 2, 1)
-        gotten(u, 1)
-        spread(part, u, 1, 1, 2, -1)
-
-    for part in (0, 1):
-        gotten(3, 0)
-        spread(part, 3, 0, 0, 1, 1)
-        gotten(1, 0)
-        spread(part, 1, 0, 1, 1, -1)
-    for part in (0, 1):
-        for u in (3, 1):
-            spread(part, u, 0, None, 2, 1)
-            spread(part, u, 0, None, 2, -1)
-    lax.fori_loop(0, 16, lend_cot, 0)
-    for part in (0, 1):
-        relay(part, 0)
-    greet(1)
-    arrived(acts_v.at[:, pl.ds(0, BLK)], ld_sem.at[0])
-    arrived(acts_v.at[:, pl.ds(BLK, BLK)], sib_recv.at[0])
-    multiply(0, 0)
-    for part in (0, 1):
-        gotten(2, 0)
-        spread(part, 2, 0, None, 2, 1)
-        spread(part, 2, 0, None, 2, -1)
-    greet(2)
-    for rx, ry in ((1, 0), (3, 0), (0, 1), (0, 3)):
-        multiply(rx, ry)
-    for u in (3, 1):
-        for part in (0, 1):
-            relay(part, u)
-    greet(3)
-    for rx, ry in ((2, 0), (0, 2), (1, 1), (1, 3), (3, 1), (3, 3)):
-        multiply(rx, ry)
-    for part in (0, 1):
-        relay(part, 2)
-    greet(4)
-    for rx, ry in ((1, 2), (3, 2), (2, 1), (2, 3), (2, 2)):
-        multiply(rx, ry)
-
-    coords_t[...] = acc[...].astype(BF16).T
-    arrived(cot_v.at[:, pl.ds(0, BLK)], ld_sem.at[1])
-    arrived(cot_v.at[:, pl.ds(BLK, BLK)], sib_recv.at[1])
-
     first = ((Y, X), (X, Y))
     WAYS = ((0, 1), (1, -1))
     order = (2, 1, 3, 0)
@@ -192,18 +174,11 @@
     def rs_slot(part, u, v):
         return (v % 4) * 4 + u % 4 if part == 0 else (u % 4) * 4 + v % 4
 
-    done = set()
-
-    def need(part, u, v):
-        s = rs_slot(part, u, v)
-        if s not in done:
-            done.add(s)
-            term_v[s] = jnp.dot(coords_t[...], cot_v[s], preferred_element_type=F32).astype(BF16)
-        return s
-
     class Run:
         def __init__(self, index, low, q, buffers):
-            self.index, self.low, self.q, self.seen = index, low, q, set()
+            self.pieces = 4 if index else 8
+            self.piece_rows = HALF // self.pieces
+            self.index, self.low, self.q, self.seen, self.done = index, low, q, set(), set()
             (
                 self.far1, self.dir1, self.comb1, self.csrc1, self.mid, self.own2,
                 self.far2, self.dir2, self.comb2, self.csrc2, self.zb, self.zrecv, self.ybuf,
@@ -223,6 +198,15 @@
             else:
                 arrived(buffer, rs_recv.at[self.index, 9 + kind])
 
+        def need(self, part, u, v):
+            s = rs_slot(part, u, v)
+            if s not in self.done:
+                self.done.add(s)
+                term_v[s, ranks[self.index], :] = jnp.dot(
+                    coords_t[self.index], cot_v[s], preferred_element_type=F32
+                ).astype(BF16)
+            return s
+
         def rows(self, part, half):
             return pl.ds(self.low + (2 * part + half) * self.q, self.q)
 
@@ -232,7 +216,7 @@
         def far(self):
             for v in order:
                 for part in (0, 1):
-                    s = need(part, 2, v)
+                    s = self.need(part, 2, v)
                     for w, way in WAYS:
                         self.send(
                             term_v.at[s, self.rows(part, w)], self.far1.at[part, w, v],
@@ -243,7 +227,7 @@
             for v in order:
                 for part in (0, 1):
                     for w, way in WAYS:
-                        s = need(part, way, v)
+                        s = self.need(part, way, v)
                         self.send(
                             term_v.at[s, self.rows(part, 1 - w)], self.dir1.at[part, w, v],
                             1, v, first[part][0], way,
@@ -315,46 +299,42 @@
                         + self.dir2[part, 1 - w].astype(F32)
                     ).astype(BF16)
                     at = (2 * part + w) * self.q
-                    if self.index == 0:
-                        self.zb[pl.ds(at, self.q), :] = total
-                    else:
-                        self.zb[pl.ds(at, self.q), :] = total[:, :128]
-                        self.zb[pl.ds(64 + at, self.q), :] = total[:, 128:]
-
-    big = Run(
-        0, 0, 48,
+                    self.zb[pl.ds(at, self.q), :] = total
+
+    run0 = Run(
+        0, 0, 32,
         (far1a, dir1a, comb1a, csrc1a, mid_a, own2a, far2a, dir2a, comb2a, csrc2a, zb_a, zrecv_a, ybuf_a),
     )
-    small = Run(
-        1, 192, 16,
+    run1 = Run(
+        1, 128, 32,
         (far1b, dir1b, comb1b, csrc1b, mid_b, own2b, far2b, dir2b, comb2b, csrc2b, zb_b, zrecv_b, ybuf_b),
     )
 
     far_first = (6, 5, 7, 4, 8, 3, 9, 2, 10, 1, 11)
 
-    def piece(run, k):
-        index = (z + k) % NZ if run.index == 0 else (z + k + 4) % NZ
-        return pl.ds(pl.multiple_of(index * 16, 16), 16), index
+    def piece(run, k, base=0):
+        zz = (z + k) % NZ
+        index = zz // 3 * 2 + zz % 3 if run.index == 0 else (zz + 2) % NZ
+        return pl.ds(pl.multiple_of(base + index * run.piece_rows, 16), run.piece_rows)
+
+    def sums(run, k=0):
+        zz = (z + k) % NZ
+        return zz % 3 != 2 if run.index == 0 else (zz + 2) % NZ < 4
 
     def owned(run, k, body):
-        if run.index == 0:
-            body()
-        else:
-            pl.when((z + k + 4) % NZ < 8)(body)
+        pl.when(sums(run, k))(body)
 
     def scatter(run):
         for k in far_first:
 
             def body(k=k):
-                at, _ = piece(run, k)
-                remote(run.zb.at[at], run.zrecv.at[k], z_sem.at[run.index, 0], z_sem.at[run.index, 1], column[k])
+                remote(run.zb.at[piece(run, k)], run.zrecv.at[k], z_sem.at[run.index, 0], z_sem.at[run.index, 1], column[k])
 
             owned(run, k, body)
 
     def swap(run):
         def body():
-            at, _ = piece(run, 0)
-            part_sum = run.zb[at, :].astype(F32)
+            part_sum = run.zb[piece(run, 0), :].astype(F32)
             arrived(run.zrecv.at[pl.ds(1, NZ - 1)], z_sem.at[run.index, 1])
             for k in range(1, NZ):
                 part_sum += run.zrecv[k].astype(F32)
@@ -363,60 +343,108 @@
 
         owned(run, 0, body)
 
-    def hand_out(run, result):
+    def settle(run):
         def body():
-            at, _ = piece(run, 0)
             arrived(run.ybuf.at[1], y_sem.at[run.index, 1])
-            result[0, at, :] = (run.ybuf[0].astype(F32) + run.ybuf[1].astype(F32)).astype(BF16)
-            for k in far_first:
-                remote(result.at[0, at], result.at[0, at], g_sem.at[run.index, 0], g_sem.at[run.index, 1], column[k])
+            g_v[0, piece(run, 0, run.low), :] = (run.ybuf[0].astype(F32) + run.ybuf[1].astype(F32)).astype(BF16)
 
         owned(run, 0, body)
 
+    def hand_out(run, places):
+        def body():
+            at = piece(run, 0, run.low)
+            for place in places:
+
+                @pl.when(z != place)
+                def _():
+                    remote(
+                        g_v.at[0, at], g_v.at[0, at], g_sem.at[run.index, 0], g_sem.at[run.index, 1],
+                        ((place * 2 + y_hi) * 2 + core, fs),
+                    )
+
+        owned(run, 0, body)
+
     def others(run, body):
-        if run.index == 0:
-            body(NZ - 1)
-        else:
-            pl.when((z + 4) % NZ < 8)(lambda: body(7))
-            pl.when((z + 4) % NZ >= 8)(lambda: body(8))
-
-    def collect(run, result):
+        pl.when(sums(run))(lambda: body(run.pieces - 1))
+        pl.when(jnp.logical_not(sums(run)))(lambda: body(run.pieces))
+
+    def collect(run):
         others(run, lambda n: arrived(run.zrecv.at[pl.ds(0, n)], g_sem.at[run.index, 1]))
-        return remote(
-            result.at[0], result.at[1], fin_sem.at[run.index, 0], fin_sem.at[run.index, 1], sibling
-        )
-
-    big.far()
-    big.direct()
-    need(0, 0, 0)
-    small.far()
-    big.combine()
-    small.direct()
+        span = pl.ds(run.low, 4 * run.q)
+        return remote(g_v.at[0, span], g_v.at[1, span], fin_sem.at[run.index, 0], fin_sem.at[run.index, 1], sibling)
+
+    gather0, gather1 = Gather(0), Gather(1)
+    SIDES = ((1, 0), (3, 0), (0, 1), (0, 3))
+    CORNERS = ((2, 0), (0, 2), (1, 1), (1, 3), (3, 1), (3, 3))
+    LAST = ((1, 2), (3, 2), (2, 1), (2, 3), (2, 2))
+    gather0.own()
+    lax.fori_loop(0, 16, load, 0)
+    greet(0)
+    lax.fori_loop(0, 16, lend, 0)
+    own_p.wait()
+    gather0.beside()
+    gather1.own()
+    gather0.relay(0)
+    greet(1)
+    gather0.opposite()
+    lax.fori_loop(0, 16, lend_cot, 0)
+    gather1.beside()
+    gather0.relay(3)
+    gather0.relay(1)
+    arrived(acts_v.at[:, pl.ds(0, BLK)], ld_sem.at[0])
+    arrived(acts_v.at[:, pl.ds(BLK, BLK)], sib_recv.at[0])
+    gather0.multiply((0, 0), *SIDES)
+    gather1.relay(0)
+    greet(2)
+    gather0.relay(2)
+    gather1.opposite()
+    gather0.multiply(*CORNERS)
+    greet(3)
+    gather0.multiply(*LAST)
+    gather0.finish()
+    gather1.relay(3)
+    gather1.relay(1)
+    arrived(cot_v.at[:, pl.ds(0, BLK)], ld_sem.at[1])
+    arrived(cot_v.at[:, pl.ds(BLK, BLK)], sib_recv.at[1])
+    run0.far()
+    gather1.relay(2)
+    run0.direct()
+    run0.need(0, 0, 0)
+    greet(4)
+    gather1.multiply((0, 0), *SIDES, *CORNERS)
+    run0.combine()
+    gather1.multiply(*LAST)
+    gather1.finish()
+    run1.far()
     greet(5)
-    big.middle()
-    small.combine()
-    big.own()
-    big.combine2()
+    run0.middle()
+    run1.direct()
+    run1.need(0, 0, 0)
+    run0.own()
+    run0.combine2()
+    run1.combine()
+    run0.total2()
+    scatter(run0)
+    run1.middle()
     lax.fori_loop(0, 16, give, 0)
-    small.middle()
-    big.total2()
-    scatter(big)
-    small.own()
-    small.combine2()
-    small.total2()
-    scatter(small)
-    swap(big)
-    swap(small)
-    hand_out(big, g_big)
-    hand_out(small, g_small)
-    tell = [collect(big, g_big), collect(small, g_small)]
+    run1.own()
+    run1.combine2()
+    run1.total2()
+    scatter(run1)
+    places = (0, 1, 2, 3, 4, 5, 11, 10, 9, 8, 7, 6)
+    for run in (run0, run1):
+        swap(run)
+        settle(run)
+        hand_out(run, places)
+    tell = [collect(run0), collect(run1)]
 
     arrived(acts_v.at[:, pl.ds(0, BLK)], sib_send.at[0])
     arrived(cot_v.at[:, pl.ds(0, BLK)], sib_send.at[1])
     arrived(p_v.at[0], osib_sem.at[0])
     arrived(p_v.at[1], osib_sem.at[1])
-    arrived(p_v.at[0, pl.ds(0, 15)], ag_send.at[0])
-    for run in (big, small):
+    for c in (0, 1):
+        arrived(p_v.at[0, pl.ds(0, 15), :, ranks[c]], ag_send.at[c])
+    for run in (run0, run1):
         for kind, buffer in enumerate((run.far1, run.dir1, run.comb1, run.far2, run.dir2, run.comb2)):
             arrived(buffer, rs_send.at[run.index, kind])
         others(run, lambda n, run=run: arrived(run.zrecv.at[pl.ds(0, n)], z_sem.at[run.index, 0]))
@@ -435,7 +463,7 @@
     hbm = pl.BlockSpec(memory_space=pltpu.HBM)
     vmem = pl.BlockSpec(memory_space=pltpu.VMEM)
 
-    def run_buffers(q, cols, pieces):
+    def run_buffers(q, piece_rows):
         first_stage = [pltpu.VMEM((2, 2, 4, q, BLK), BF16)] * 4
         second_stage = [pltpu.VMEM((2, 2, q, BLK), BF16)] * 4
         return [
@@ -443,34 +471,33 @@
             pltpu.VMEM((2, 4, 2 * q, BLK), BF16),
             pltpu.VMEM((2, 2 * q, BLK), F32),
             *second_stage,
-            pltpu.VMEM((pieces * 16, cols), BF16),
-            pltpu.VMEM((NZ, 16, cols), BF16),
-            pltpu.VMEM((2, 16, cols), BF16),
+            pltpu.VMEM((4 * q, BLK), BF16),
+            pltpu.VMEM((NZ, piece_rows, BLK), BF16),
+            pltpu.VMEM((2, piece_rows, BLK), BF16),
         ]
 
     return pl.pallas_call(
         gather_reduce,
         out_shape=(
             pltpu.VMEM((2, 16, BLK, BLK), BF16),
-            pltpu.VMEM((2, 192, BLK), BF16),
-            pltpu.VMEM((2, 128, 128), BF16),
+            pltpu.VMEM((2, BLK, BLK), BF16),
         ),
         in_specs=[hbm] * 3,
-        out_specs=(vmem, vmem, vmem),
+        out_specs=(vmem, vmem),
         scratch_shapes=[
             pltpu.VMEM((16, 512, BLK), BF16),
             pltpu.VMEM((16, 512, BLK), BF16),
-            pltpu.VMEM((512, BLK), F32),
-            pltpu.VMEM((BLK, 512), BF16),
+            pltpu.VMEM((2, 512, HALF), F32),
+            pltpu.VMEM((2, HALF, 512), BF16),
             pltpu.VMEM((16, BLK, BLK), BF16),
-            *run_buffers(48, BLK, 12),
-            *run_buffers(16, 128, 8),
+            *run_buffers(32, 16),
+            *run_buffers(32, 32),
             pltpu.SemaphoreType.REGULAR((5,)),
             dma((3,)),
             dma((2,)),
             dma((2,)),
-            dma((1,)),
-            dma((13,)),
+            dma((2,)),
+            dma((2, 13)),
             dma((2,)),
             dma((2, 6)),
             dma((2, 15)),
@@ -486,17 +513,14 @@
     )(acts, cotangent, projector)
 
 
-def update_kernel(p, g_big, g_small, m1, m2, first_new, second_new, update, first_v, second_v, dir_t, update_v, sems):
+def update_kernel(p, g_v, m1, m2, first_new, second_new, update, first_v, second_v, dir_t, update_v, sems):
     core = lax.axis_index("dp") % 2
     fs = lax.axis_index("fsdp")
     x, y_lo = fs // NYL, fs % NYL
     first_fix = 1.0 - 0.9**STEP
     second_fix = 1.0 - 0.999**STEP
     for half in range(2):
-        small = g_small[half]
-        low = jnp.concatenate(
-            [g_big[half], jnp.concatenate([small[:64], small[64:]], axis=1)], axis=0
-        ).astype(F32).T
+        low = g_v[half].astype(F32).T
         which = core if half == 0 else 1 - core
         cols = pl.ds(pl.multiple_of(which * BLK, BLK), BLK)
         first = 0.9 * m1[:, cols] + 0.1 * low
@@ -523,7 +547,7 @@
     pltpu.make_async_copy(update_v, update_v, sems.at[2]).wait()
 
 
-def adam_and_update(p, g_big, g_small, first_moment, second_moment):
+def adam_and_update(p, g_v, first_moment, second_moment):
     vmem = pl.BlockSpec(memory_space=pltpu.VMEM)
     return pl.pallas_call(
         update_kernel,
@@ -532,7 +556,7 @@
             jax.ShapeDtypeStruct((BLK, 512), F32),
             jax.ShapeDtypeStruct((4096, BLK), F32),
         ),
-        in_specs=[vmem] * 5,
+        in_specs=[vmem] * 4,
         out_specs=(pl.BlockSpec(memory_space=pl.ANY),) * 3,
         scratch_shapes=[
             pltpu.VMEM((BLK, 512), F32),
@@ -543,14 +567,14 @@
         ],
         compiler_params=pltpu.CompilerParams(vmem_limit_bytes=40 << 20),
         name="adam_and_update",
-    )(p, g_big, g_small, first_moment, second_moment)
+    )(p, g_v, first_moment, second_moment)
 
 
 def on_device(acts, cotangent, projector, first_moment, second_moment):
-    p, g_big, g_small = gather_and_sum(
+    p, g_v = gather_and_sum(
         *(pltpu.with_memory_space_constraint(a, pltpu.HBM) for a in (acts, cotangent, projector))
     )
-    return adam_and_update(p, g_big, g_small, first_moment, second_moment)
+    return adam_and_update(p, g_v, first_moment, second_moment)
 
 
 def solution(mesh):

time: 76.4 us -> 75 us (0.982)
  Pallas kernels: 75.6 us -> 74.2 us
    pallas_call x1, Pallas kernels: 72.7 us -> 71.3 us  [gather_and_sum(): pl.pallas_call(gather_reduce, out_shape=(pltpu.VMEM((2, 16, BLK, BLK), BF...]
where the time goes in v3:
time: 75 us; the launch traced here: 74.9 us
  Pallas kernels  74.2 us (99%)
    pallas_call x1, Pallas kernels, gather_and_sum(): pl.pallas_call(gather_reduce, out_shape=(pltpu.VMEM((2, 16, BLK, BLK), BF...  71.3 us
    pallas_call x1, Pallas kernels, adam_and_update(): pl.pallas_call(update_kernel, out_shape=(jax.ShapeDtypeStruct((BLK, 512),...  2.95 us

profile of v3, /device:TPU:1, one launch (start us, length us, event | category | flops | bytes accessed | tf_op | source)
XLA Modules:
  0.0 74.9 jit_solution(4041192081840723284)
XLA Ops:
  0.6 0.0 copy-start.1
  0.6 0.0 copy-start
  0.7 71.3 %gather_and_sum.1 = (bf16[2,16,256,256]{3,2,1,0:T(8,128)(2,1)S(1)}, bf16[2,256,256]{2,1,0:T(8,128)(2,1)S(1)}) custom-call(bf16[256,4096]{1,0:T(8,128)(2,1)} %acts.1, bf16[256,4096]{1,0:T(8,128)(2,1)} %cot.1, bf16[256,512]{1,0:T(8,128)(2,1)} %proj.1), custom_call_target="tpu_custom_call" | custom-call | tf_op jit(solution)/shard_map/gather_and_sum/pallas_call | solution.py:479
  71.9 0.0 copy-done.1
  72.0 0.0 copy-done
  72.0 2.9 %adam_and_update.1 = (f32[256,512]{1,0:T(8,128)}, f32[256,512]{1,0:T(8,128)}, f32[4096,256]{1,0:T(8,128)}) custom-call(bf16[2,16,256,256]{3,2,1,0:T(8,128)(2,1)S(1)} %get-tuple-element.5.p, bf16[2,256,256]{2,1,0:T(8,128)(2,1)S(1)} %get-tuple-element.6.g_v, f32[256,512]{1,0:T(8,128)S(1)} %copy-done, f32[256,512]{1,0:T(8,128)S(1)} %copy-done.1), custom_call_target="tpu_custom_call" | custom-call | tf_op jit(solution)/shard_map/adam_and_update/pallas_call | solution.py:552
Async XLA Ops:
  0.6 71.3 %copy-start.1 = (f32[256,512]{1,0:T(8,128)S(1)}, f32[256,512]{1,0:T(8,128)}, u32[]{:S(2)}) copy-start(f32[256,512]{1,0:T(8,128)} %m2.1) | copy-start | bytes 1572868
  0.6 71.3 %copy-start = (f32[256,512]{1,0:T(8,128)S(1)}, f32[256,512]{1,0:T(8,128)}, u32[]{:S(2)}) copy-start(f32[256,512]{1,0:T(8,128)} %m1.1) | copy-start | bytes 1572868

commit v4 on v3

--- a/solution.py
+++ b/solution.py
@@ -426,11 +426,11 @@
     run0.total2()
     scatter(run0)
     run1.middle()
-    lax.fori_loop(0, 16, give, 0)
     run1.own()
     run1.combine2()
     run1.total2()
     scatter(run1)
+    lax.fori_loop(0, 16, give, 0)
     places = (0, 1, 2, 3, 4, 5, 11, 10, 9, 8, 7, 6)
     for run in (run0, run1):
         swap(run)

time: 75 us -> 75.1 us (level)
  no operation moved by 1% of the time
where the time goes in v4:
time: 75.1 us; the launch traced here: 75 us
  Pallas kernels  74.3 us (99%)
    pallas_call x1, Pallas kernels, gather_and_sum(): pl.pallas_call(gather_reduce, out_shape=(pltpu.VMEM((2, 16, BLK, BLK), BF...  71.4 us
    pallas_call x1, Pallas kernels, adam_and_update(): pl.pallas_call(update_kernel, out_shape=(jax.ShapeDtypeStruct((BLK, 512),...  2.95 us

profile of v4, /device:TPU:1, one launch (start us, length us, event | category | flops | bytes accessed | tf_op | source)
XLA Modules:
  0.0 75.0 jit_solution(10246738101074404076)
XLA Ops:
  0.6 0.0 copy-start.1
  0.6 0.0 copy-start
  0.7 71.4 %gather_and_sum.1 = (bf16[2,16,256,256]{3,2,1,0:T(8,128)(2,1)S(1)}, bf16[2,256,256]{2,1,0:T(8,128)(2,1)S(1)}) custom-call(bf16[256,4096]{1,0:T(8,128)(2,1)} %acts.1, bf16[256,4096]{1,0:T(8,128)(2,1)} %cot.1, bf16[256,512]{1,0:T(8,128)(2,1)} %proj.1), custom_call_target="tpu_custom_call" | custom-call | tf_op jit(solution)/shard_map/gather_and_sum/pallas_call | solution.py:479
  72.0 0.0 copy-done.1
  72.0 0.0 copy-done
  72.1 2.9 %adam_and_update.1 = (f32[256,512]{1,0:T(8,128)}, f32[256,512]{1,0:T(8,128)}, f32[4096,256]{1,0:T(8,128)}) custom-call(bf16[2,16,256,256]{3,2,1,0:T(8,128)(2,1)S(1)} %get-tuple-element.5.p, bf16[2,256,256]{2,1,0:T(8,128)(2,1)S(1)} %get-tuple-element.6.g_v, f32[256,512]{1,0:T(8,128)S(1)} %copy-done, f32[256,512]{1,0:T(8,128)S(1)} %copy-done.1), custom_call_target="tpu_custom_call" | custom-call | tf_op jit(solution)/shard_map/adam_and_update/pallas_call | solution.py:552
Async XLA Ops:
  0.6 71.4 %copy-start.1 = (f32[256,512]{1,0:T(8,128)S(1)}, f32[256,512]{1,0:T(8,128)}, u32[]{:S(2)}) copy-start(f32[256,512]{1,0:T(8,128)} %m2.1) | copy-start | bytes 1572868
  0.6 71.4 %copy-start = (f32[256,512]{1,0:T(8,128)S(1)}, f32[256,512]{1,0:T(8,128)}, u32[]{:S(2)}) copy-start(f32[256,512]{1,0:T(8,128)} %m1.1) | copy-start | bytes 1572868
